TPU v7x, 32 devices: a whole 2x2x4 slice. The times are simulated.
32 devices in a mesh: slab: 4 (over x, core), dom: 8 (over z, y).
Axes of the slice: x: 2, y: 2, z: 4, core: 2. Of those that a mesh axis runs over, the one named last changes fastest.
Arguments:
- coords: float32 [3, 4, 8, 512], P(None, 'slab', 'dom'), may hold values from -6 to 6
- velocity: float32 [3, 4, 8, 512], P(None, 'slab', 'dom'), may hold values from -6 to 6
- charge: float32 [4, 8, 512], P('slab', 'dom'), may hold values from -1 to 1
- inv_mass: float32 [4, 8, 512], P('slab', 'dom'), may hold values from 0.0625 to 1
- tile_block: int32 [4, 8, 64], P('slab', 'dom'), may hold values from 0 to 3
- tile_atoms: int32 [4, 8, 64, 128], P('slab', 'dom'), may hold values from 0 to 2047
- active_tile_count: int32 [4, 8], P('slab', 'dom'), may hold values from 1 to 64
- bond_atoms: int32 [2, 4, 8, 256], P(None, 'slab', 'dom'), may hold values from 0 to 511, as said below
- cross_atoms: int32 [2, 4, 8, 128], P(None, 'slab', 'dom'), may hold values from 0 to 255
- cross_side: int32 [4, 8, 128], P('slab', 'dom'), may hold values from 0 to 3
- cross_count: int32 [4, 8], P('slab', 'dom'), may hold values from 1 to 128
Outputs:
- coords_out: float32 [3, 4, 8, 512], P(None, 'slab', 'dom')
- velocity_out: float32 [3, 4, 8, 512], P(None, 'slab', 'dom')
Inputs may be any that keep to these rules, and one draw needn't show every extreme that they name: `bond_atoms`: each bond joins two different atoms of the domain that holds it. `cross_atoms`: row 0 is an atom of the owning domain, row 1 an atom of the neighbour named by cross_side; both are among the first 256 atoms of their domains. `cross_side`: codes 0 to 3 name the in-slab neighbours at offsets +1, -1, +2, -2 along dom, cyclically. `cross_count`: slots below the count are live. `active_tile_count`: tiles below the count are live. `tile_atoms`: entries index the domain's halo list as in the first step.
All inputs are finite; a program needn't handle non-finite values.
Results may differ from a plain program's by a relative error of at most 0.0003.
Values sent between devices are 32-bit elements; how exact they have to be, the bound alone decides.
No kernel may reach another device: no remote copies, remote signals or barrier semaphores. Data moves between devices by JAX's collectives and lax.ppermute only.
A program may use at most 64 MiB of HBM per device.

v0:
```python
import functools

import jax
import jax.numpy as jnp
from jax import lax
from jax.experimental import pallas as pl
from jax.experimental.pallas import tpu as pltpu
from jax.sharding import PartitionSpec as P

TILE = 128
ORDER = 4
LANES = 128
SUBLANES = 8

time_step = 0.1
cutoff_sq = 16.0
force_scale = 4.0
length_floor = 0.25


def passed_along(array, axis, by):
    length = lax.axis_size(axis)
    return lax.ppermute(array, axis, [(i, (i + by) % length) for i in range(length)])


def strides_of(domains):
    row_width = max(2, domains // 8)
    return (1, -1, row_width, -row_width)


def round_up(count, step):
    return -(-count // step) * step


class Rows:
    def __init__(self, atoms, bonds, slots):
        self.atom_rows = atoms // LANES
        self.shell_rows = atoms // 2 // LANES
        self.bond_rows = bonds // LANES
        self.slot_rows = slots // LANES
        at = 0
        self.coords = []
        for _ in range(3):
            self.coords.append(at)
            at += self.atom_rows
        self.charge = at
        at += self.atom_rows
        self.mass = at
        at += self.atom_rows
        self.bond_first = at
        at += self.bond_rows
        self.bond_second = at
        at += self.bond_rows
        self.cross_first = at
        at += self.slot_rows
        self.cross_second = at
        at += self.slot_rows
        self.side = at
        at += self.slot_rows
        self.live = at
        at += self.slot_rows
        self.used = at
        self.count = round_up(at, SUBLANES)
        self.shell_terms = (self.bond_rows + self.slot_rows) * LANES
        self.inner_at = (0, self.shell_terms)
        self.cross_at = self.bond_rows * LANES
        self.far_at = self.shell_terms + self.bond_rows * LANES
        self.matrix = self.far_at + self.slot_rows * LANES
        self.disp_used = 3 * self.atom_rows
        self.disp_count = round_up(self.disp_used, SUBLANES)


def take_lanes(table, lanes):
    return jnp.take_along_axis(table, lanes, axis=1, mode="promise_in_bounds")


def pick(tables, index):
    lanes = index & (LANES - 1)
    chunk = index >> 7
    result = take_lanes(tables[0], lanes)
    for k in range(1, len(tables)):
        result = jnp.where(chunk == k, take_lanes(tables[k], lanes), result)
    return result


def fetched(sources, targets, sem_ref):
    copies = [pltpu.make_async_copy(s, t, sem_ref.at[n]) for n, (s, t) in enumerate(zip(sources, targets))]
    for copy in copies:
        copy.start()
    return copies


def pack_kernel(rows, copies, count_ref, *refs):
    sources, (out_ref, rim_ref), targets, sem_ref = refs[:6], refs[6:8], refs[8:14], refs[14]
    for copy in fetched(sources, targets, sem_ref):
        copy.wait()
    coords_ref, charge_ref, mass_ref, bonds_ref, cross_ref, side_ref = targets

    def put(row, value):
        for part in range(value.shape[1] // LANES):
            piece = value[:, part * LANES : (part + 1) * LANES]
            for copy in range(copies):
                out_ref[pl.ds(copy * rows.count + row + part, 1), :] = piece

    shell = rows.shell_rows * LANES
    fields = [coords_ref[c, 0] for c in range(3)] + [charge_ref[0]]
    for c in range(4):
        at = rows.coords[c] if c < 3 else rows.charge
        put(at, fields[c])
        for part in range(rows.shell_rows):
            rim_ref[pl.ds(c * rows.shell_rows + part, 1), :] = fields[c][:, part * LANES : (part + 1) * LANES]
    put(rows.mass, mass_ref[0])
    put(rows.bond_first, bonds_ref[0, 0].astype(jnp.float32))
    put(rows.bond_second, bonds_ref[1, 0].astype(jnp.float32))
    put(rows.cross_first, cross_ref[0, 0].astype(jnp.float32))
    put(rows.cross_second, cross_ref[1, 0].astype(jnp.float32))
    side = side_ref[0]
    put(rows.side, side.astype(jnp.float32))
    slot = lax.broadcasted_iota(jnp.int32, side.shape, 1)
    put(rows.live, jnp.where(slot < count_ref[0, 0], 1.0, 0.0))
    if rows.count > rows.used:
        for copy in range(copies):
            out_ref[pl.ds(copy * rows.count + rows.used, rows.count - rows.used), :] = jnp.zeros(
                (rows.count - rows.used, LANES), jnp.float32
            )


SHRINK = 1.0 / 4.0
OUT_OF_REACH = 1000.0
TILES_STEP = 2


def own_kernel(
    rows,
    coords_hbm,
    charge_hbm,
    velocity_hbm,
    mass_hbm,
    atoms_hbm,
    own_ref,
    far_ref,
    index_ref,
    motion_ref,
    coords_ref,
    charge_ref,
    velocity_ref,
    mass_ref,
    sem_ref,
):
    atom_rows = rows.atom_rows
    copies = fetched(
        (coords_hbm, charge_hbm, atoms_hbm.at[0, 0], velocity_hbm, mass_hbm),
        (coords_ref, charge_ref, index_ref, velocity_ref, mass_ref),
        sem_ref,
    )
    down = lax.broadcasted_iota(jnp.int32, (SUBLANES, LANES), 0)
    copies[0].wait()
    copies[1].wait()

    def lanes_of(part):
        return slice(part * LANES, (part + 1) * LANES)

    table = []
    for c in range(4):
        field = coords_ref[c, 0] * SHRINK if c < 3 else charge_ref[0]
        table.append(
            [jnp.broadcast_to(field[:, lanes_of(part)], (SUBLANES, LANES)) for part in range(atom_rows)]
        )
    for part in range(atom_rows):
        for group in range(LANES // SUBLANES):
            at = part * LANES + group * SUBLANES
            for c in range(4):
                value = take_lanes(table[c][part], down + group * SUBLANES)
                own_ref[c, pl.ds(at, SUBLANES), :] = value if c < 3 else value * 8.0
    copies[2].wait()
    for group in range(index_ref.shape[0] // SUBLANES):
        at = pl.ds(group * SUBLANES, SUBLANES)
        index = index_ref[at, :]
        for c in range(4):
            far_ref[c, at, :] = pick(table[c], index)
    copies[3].wait()
    copies[4].wait()
    fields = [velocity_ref[c, 0] for c in range(3)] + [mass_ref[0]]
    for c, field in enumerate(fields):
        for part in range(atom_rows):
            motion_ref[pl.ds(c * atom_rows + part, 1), :] = field[:, lanes_of(part)]


def force_kernel(
    rows,
    copies,
    holders,
    here_ref,
    live_ref,
    block_hbm,
    around_ref,
    below_ref,
    above_ref,
    own_ref,
    near_ref,
    index_ref,
    motion_ref,
    out_ref,
    table_ref,
    far_ref,
    sum_ref,
    block_ref,
    sem_ref,
):
    atom_rows, shell_rows = rows.atom_rows, rows.shell_rows
    tiles = index_ref.shape[0]
    block_copy = pltpu.make_async_copy(block_hbm, block_ref, sem_ref)
    block_copy.start()
    me = here_ref[0]
    starts = [rows.coords[0], rows.coords[1], rows.coords[2], rows.charge]
    entry_rows = 6 * shell_rows
    blocks = around_ref.shape[0] // rows.count

    def broadcast(row):
        return jnp.broadcast_to(row, (SUBLANES, LANES))

    for c in range(4):
        factor = SHRINK if c < 3 else 1.0
        at = 0
        for neighbour in range(4):
            base = lax.rem(me + holders[neighbour], blocks) * rows.count + starts[c]
            for part in range(shell_rows):
                table_ref[c, at] = broadcast(around_ref[pl.ds(base + part, 1), :] * factor)
                at += 1
        for slab_ref in (below_ref, above_ref):
            for part in range(shell_rows):
                table_ref[c, at] = broadcast(slab_ref[pl.ds(c * shell_rows + part, 1), :] * factor)
                at += 1

    live = live_ref[0, 0]
    down = lax.broadcasted_iota(jnp.int32, (SUBLANES, LANES), 0)
    for group in range(tiles // SUBLANES):
        at = pl.ds(group * SUBLANES, SUBLANES)
        index = index_ref[at, :]
        lanes = index & (LANES - 1)
        chunk = index >> 7
        values = [near_ref[c, at, :] for c in range(4)]
        for k in range(entry_rows):
            here = chunk == atom_rows + k
            values = [jnp.where(here, take_lanes(table_ref[c, k], lanes), values[c]) for c in range(4)]
        values[0] = jnp.where(down + group * SUBLANES < live, values[0], OUT_OF_REACH)
        for c in range(4):
            far_ref[c, at, :] = values[c]

    sum_ref[...] = jnp.zeros(sum_ref.shape, jnp.float32)
    block_copy.wait()

    def add_tile(tile):
        base = block_ref[0, 0, tile] * TILE
        far = [broadcast(far_ref[c, pl.ds(tile, 1), :]) for c in range(4)]
        for group in range(TILE // SUBLANES):
            at = pl.ds(pl.multiple_of(base + group * SUBLANES, SUBLANES), SUBLANES)
            gap = [own_ref[c, at, :] - far[c] for c in range(3)]
            square = gap[0] * gap[0] + gap[1] * gap[1] + gap[2] * gap[2]
            inverse = pl.reciprocal(square + 1.0 / cutoff_sq, approx=True)
            weight = inverse * jnp.maximum(1.0 - square, 0.0)
            strength = (inverse - own_ref[3, at, :] * far[3]) * (weight * weight)
            for c in range(3):
                sum_ref[c, at, :] = sum_ref[c, at, :] + strength * gap[c]

    def add_tiles(step, _):
        for n in range(TILES_STEP):
            add_tile(step * TILES_STEP + n)
        return 0

    lax.fori_loop(0, lax.div(live + TILES_STEP - 1, TILES_STEP), add_tiles, 0)

    scale = time_step * time_step * force_scale * 4.0 / 2048.0

    def lane_sums(c, part):
        return jnp.sum(sum_ref[c, pl.ds(part * LANES, LANES), :].T, axis=0, keepdims=True)

    for part in range(atom_rows):
        mass = motion_ref[pl.ds(3 * atom_rows + part, 1), :]
        for c in range(3):
            speed = motion_ref[pl.ds(c * atom_rows + part, 1), :]
            moved = time_step * speed + scale * lane_sums(c, part) * mass
            for copy in range(copies):
                out_ref[pl.ds(copy * rows.disp_count + c * atom_rows + part, 1), :] = moved
    if rows.disp_count > rows.disp_used:
        for copy in range(copies):
            out_ref[pl.ds(copy * rows.disp_count + rows.disp_used, rows.disp_count - rows.disp_used), :] = jnp.zeros(
                (rows.disp_count - rows.disp_used, LANES), jnp.float32
            )


def bond_kernel(rows, domains, strides, around_ref, weight_ref, matrix_ref):
    atom_rows, shell_rows = rows.atom_rows, rows.shell_rows

    def load(row):
        return around_ref[pl.ds(row, domains, stride=rows.count), :]

    def index(row):
        return load(row).astype(jnp.int32)

    fields = [[load(at + part) for part in range(atom_rows)] for at in rows.coords + [rows.mass]]

    def weights(first, second, row):
        gap = [first[c] - second[c] for c in range(3)]
        length_sq = gap[0] * gap[0] + gap[1] * gap[1] + gap[2] * gap[2] + length_floor
        scale = lax.rsqrt(length_sq) * lax.rsqrt(first[3] + second[3])
        return [gap[c] * scale for c in range(3)]

    at = 0
    for part in range(rows.bond_rows):
        first = index(rows.bond_first + part)
        second = index(rows.bond_second + part)
        values = weights([pick(f, first) for f in fields], [pick(f, second) for f in fields], at)
        for c in range(3):
            weight_ref[pl.ds((at * 3 + c) * domains, domains), :] = values[c]
        at += 1
    for part in range(rows.slot_rows):
        first = index(rows.cross_first + part)
        second = index(rows.cross_second + part)
        side = load(rows.side + part)
        live = load(rows.live + part)
        other = [jnp.zeros((domains, LANES), jnp.float32) for _ in range(4)]
        for code, stride in enumerate(strides):
            seen = pltpu.roll(second, stride % domains, 0)
            for f in range(4):
                value = pltpu.roll(pick(fields[f][:shell_rows], seen), -stride % domains, 0)
                other[f] = jnp.where(side == code, value, other[f])
        values = weights([pick(f[:shell_rows], first) for f in fields], other, at)
        for c in range(3):
            weight_ref[pl.ds((at * 3 + c) * domains, domains), :] = values[c] * live
        at += 1

    down = lax.broadcasted_iota(jnp.int32, (SUBLANES, LANES), 0)
    group_rows = 4 * SUBLANES

    kind = jnp.bfloat16 if shell_rows * LANES <= 256 else jnp.float32
    across = lax.broadcasted_iota(jnp.int32, (group_rows, LANES), 1).astype(jnp.float32)
    lanes = [(across + float(block * LANES)).astype(kind) for block in range(shell_rows)]

    def column(row, step, half=0):
        row = jnp.broadcast_to(row, (SUBLANES, LANES))
        groups = [take_lanes(row, down + at) for at in range(step * group_rows, (step + 1) * group_rows, SUBLANES)]
        return (jnp.concatenate(groups, axis=0) - float(half * shell_rows * LANES)).astype(kind)

    def put(at, ends, signs):
        for block in range(shell_rows):
            value = jnp.zeros((group_rows, LANES), kind)
            for end, sign in zip(ends, signs):
                value = jnp.where(end == lanes[block], jnp.full((group_rows, LANES), sign, kind), value)
            matrix_ref[pl.ds(at, group_rows), block * LANES : (block + 1) * LANES] = value.astype(matrix_ref.dtype)

    def build(domain, _):
        start = pl.multiple_of(domain * rows.matrix, LANES)
        for part in range(rows.bond_rows):
            first = around_ref[pl.ds(domain * rows.count + rows.bond_first + part, 1), :]
            second = around_ref[pl.ds(domain * rows.count + rows.bond_second + part, 1), :]
            for step in range(LANES // group_rows):
                for half in range(2):
                    ends = (column(first, step, half), column(second, step, half))
                    put(start + rows.inner_at[half] + part * LANES + step * group_rows, ends, (1.0, -1.0))
        for part in range(rows.slot_rows):
            for row_at, to, sign in (
                (rows.cross_first, rows.cross_at, 1.0),
                (rows.cross_second, rows.far_at, -1.0),
            ):
                row = around_ref[pl.ds(domain * rows.count + row_at + part, 1), :]
                for step in range(LANES // group_rows):
                    put(start + to + part * LANES + step * group_rows, (column(row, step),), (sign,))
        return 0

    lax.fori_loop(0, domains, build, 0)


def solve_kernel(
    rows,
    domains,
    strides,
    here_ref,
    around_ref,
    moves_ref,
    weight_ref,
    matrix_ref,
    coords_out_ref,
    velocity_out_ref,
    push_ref,
    far_push_ref,
    field_ref,
):
    atom_rows, shell_rows = rows.atom_rows, rows.shell_rows
    bond_rows, slot_rows = rows.bond_rows, rows.slot_rows
    me = here_ref[0]

    def load(row):
        return around_ref[pl.ds(row, domains, stride=rows.count), :]

    def index(row):
        return load(row).astype(jnp.int32)

    inner_first = [index(rows.bond_first + p) for p in range(bond_rows)]
    inner_second = [index(rows.bond_second + p) for p in range(bond_rows)]
    cross_first = [index(rows.cross_first + p) for p in range(slot_rows)]
    cross_second = [index(rows.cross_second + p) for p in range(slot_rows)]
    sides = [load(rows.side + p) for p in range(slot_rows)]
    masses = [load(rows.mass + p) for p in range(atom_rows)]

    def weight(at, c):
        return weight_ref[pl.ds((at * 3 + c) * domains, domains), :]

    def project(fields):
        result = []
        for part in range(bond_rows):
            total = 0.0
            for c in range(3):
                ends = pick(fields[c], inner_first[part]) - pick(fields[c], inner_second[part])
                total = total + weight(part, c) * ends
            result.append(total)
        for part in range(slot_rows):
            seen = [pltpu.roll(cross_second[part], stride % domains, 0) for stride in strides]
            total = 0.0
            for c in range(3):
                shell = fields[c][:shell_rows]
                other = 0.0
                for code, stride in enumerate(strides):
                    value = pltpu.roll(pick(shell, seen[code]), -stride % domains, 0)
                    other = jnp.where(sides[part] == code, value, other)
                total = total + weight(bond_rows + part, c) * (pick(shell, cross_first[part]) - other)
            result.append(total)
        return result

    def put_pushes(values):
        for at, value in enumerate(values):
            for c in range(3):
                pushed = weight(at, c) * value
                high = pushed.astype(jnp.bfloat16).astype(jnp.float32)
                for row, part in ((c, high), (3 + c, pushed - high)):
                    push_ref[at, pl.ds(row * domains, domains), :] = part
                    if at >= bond_rows:
                        for code in range(4):
                            far_push_ref[at - bond_rows, pl.ds((code * SUBLANES + row) * domains, domains), :] = (
                                jnp.where(sides[at - bond_rows] == code, part, 0.0)
                            )

    def pushes_of(at, domain):
        return push_ref[at, pl.ds(domain, SUBLANES, stride=domains), :].astype(jnp.bfloat16)

    def product(pushes, domain, at):
        start = domain * rows.matrix + at
        if not isinstance(start, int):
            start = pl.multiple_of(start, LANES)
        pushes = pushes[0] if len(pushes) == 1 else jnp.concatenate(pushes, axis=1)
        result = jnp.dot(
            pushes, matrix_ref[pl.ds(start, pushes.shape[1]), :], preferred_element_type=jnp.float32
        )
        return [result[:, p * LANES : (p + 1) * LANES] for p in range(shell_rows)]

    def inner_totals(domain):
        pushes = [pushes_of(at, domain) for at in range(bond_rows + slot_rows)]
        return product(pushes, domain, 0) + product(pushes[:bond_rows], domain, rows.shell_terms)

    def far_totals(domain, first_row, count):
        pushes = [
            far_push_ref[p, pl.ds(first_row * domains + domain, count, stride=domains), :].astype(jnp.bfloat16)
            for p in range(slot_rows)
        ]
        return product(pushes, domain, rows.far_at)

    def spread(values):
        put_pushes(values)
        for domain in range(domains):
            for part, total in enumerate(inner_totals(domain)):
                field_ref[0, part, pl.ds(domain, SUBLANES, stride=domains), :] = total
            for part, total in enumerate(far_totals(domain, 0, 4 * SUBLANES)):
                for code, stride in enumerate(strides):
                    field_ref[1 + code, part, pl.ds((domain + stride) % domains, SUBLANES, stride=domains), :] = total[
                        code * SUBLANES : (code + 1) * SUBLANES, :
                    ]

        def field(c, part):
            pieces = [
                field_ref[source, part, pl.ds(row * domains, domains), :]
                for source in range(5 if part < shell_rows else 1)
                for row in (c, 3 + c)
            ]
            return masses[part] * functools.reduce(lambda a, b: a + b, pieces)

        return [[field(c, part) for part in range(atom_rows)] for c in range(3)]

    moves = [
        [moves_ref[pl.ds(c * atom_rows + p, domains, stride=rows.disp_count), :] for p in range(atom_rows)]
        for c in range(3)
    ]
    push_ref[...] = jnp.zeros(push_ref.shape, jnp.float32)
    far_push_ref[...] = jnp.zeros(far_push_ref.shape, jnp.float32)
    residue = project(moves)

    def expand(_, carry):
        residue, summed = carry
        change = project(spread(residue))
        residue = [now - step for now, step in zip(residue, change)]
        return residue, [a + b for a, b in zip(summed, residue)]

    residue, summed = lax.fori_loop(0, ORDER, expand, (residue, residue))
    put_pushes(summed)
    sums = inner_totals(me)
    for code, stride in enumerate(strides):
        owner = lax.rem(me + (-stride) % domains, domains)
        for part, total in enumerate(far_totals(owner, code * SUBLANES, SUBLANES)):
            sums[part] = sums[part] + total
    for part in range(atom_rows):
        lanes = slice(part * LANES, (part + 1) * LANES)
        mass = around_ref[pl.ds(me * rows.count + rows.mass + part, 1), :]
        for c in range(3):
            correction = mass * (sums[part][c : c + 1, :] + sums[part][3 + c : 4 + c, :])
            move = moves_ref[pl.ds(me * rows.disp_count + c * atom_rows + part, 1), :] - correction
            start = around_ref[pl.ds(me * rows.count + rows.coords[c] + part, 1), :]
            coords_out_ref[c, 0, :, lanes] = start + move
            velocity_out_ref[c, 0, :, lanes] = move * (1.0 / time_step)


def vmem(count):
    return [pl.BlockSpec(memory_space=pltpu.VMEM)] * count


def smem(count):
    return [pl.BlockSpec(memory_space=pltpu.SMEM)] * count


def hbm(count):
    return [pl.BlockSpec(memory_space=pltpu.HBM)] * count


def in_hbm(arrays):
    return [pltpu.with_memory_space_constraint(a, pltpu.HBM) for a in arrays]


def params(mebibytes):
    return pltpu.CompilerParams(vmem_limit_bytes=mebibytes * 1024 * 1024)


def cost(flops, moved):
    return pl.CostEstimate(flops=flops, bytes_accessed=moved, transcendentals=0)


def room_for(arrays):
    return [pltpu.VMEM(a.shape, a.dtype) for a in arrays]


def shards(
    coords,
    velocity,
    charge,
    inv_mass,
    tile_block,
    tile_atoms,
    active_tile_count,
    bond_atoms,
    cross_atoms,
    cross_side,
    cross_count,
):
    atoms = coords.shape[-1]
    tiles = tile_atoms.shape[2]
    domains = lax.axis_size("dom")
    strides = strides_of(domains)
    rows = Rows(atoms, bond_atoms.shape[-1], cross_side.shape[-1])
    whole_slab = domains == SUBLANES
    copies = domains if whole_slab else 1
    f32 = jnp.float32

    sent = (coords, charge, inv_mass, bond_atoms, cross_atoms, cross_side)
    packed, rim = pl.pallas_call(
        functools.partial(pack_kernel, rows, copies),
        out_shape=(
            jax.ShapeDtypeStruct((copies * rows.count, LANES), f32),
            jax.ShapeDtypeStruct((4 * rows.shell_rows, LANES), f32),
        ),
        in_specs=smem(1) + hbm(len(sent)),
        out_specs=tuple(vmem(2)),
        scratch_shapes=room_for(sent) + [pltpu.SemaphoreType.DMA((len(sent),))],
        compiler_params=params(4),
        name="pack",
    )(cross_count, *in_hbm(sent))

    alone = (coords, charge, velocity, inv_mass, tile_atoms)
    own = pl.pallas_call(
        functools.partial(own_kernel, rows),
        out_shape=(
            jax.ShapeDtypeStruct((4, atoms, LANES), f32),
            jax.ShapeDtypeStruct((4, tiles, TILE), f32),
            jax.ShapeDtypeStruct((tiles, TILE), jnp.int32),
            jax.ShapeDtypeStruct((4 * rows.atom_rows, LANES), f32),
        ),
        in_specs=hbm(len(alone)),
        out_specs=tuple(vmem(4)),
        scratch_shapes=room_for(alone[:4]) + [pltpu.SemaphoreType.DMA((len(alone),))],
        compiler_params=params(4),
        cost_estimate=cost(64 * atoms * LANES, 16 * atoms * LANES),
        name="own",
    )(*in_hbm(alone))

    below = passed_along(rim, "slab", 1)
    above = passed_along(rim, "slab", -1)
    if whole_slab:
        around = lax.all_to_all(packed, "dom", 0, 0, tiled=True)
        here = lax.axis_index("dom").reshape(1)
        holders = [stride % domains for stride in strides]
    else:
        around = jnp.concatenate([packed] + [passed_along(packed, "dom", -stride) for stride in strides], axis=0)
        here = jnp.zeros(1, jnp.int32)
        holders = [1, 2, 3, 4]

    moves = pl.pallas_call(
        functools.partial(force_kernel, rows, copies, holders),
        out_shape=jax.ShapeDtypeStruct((copies * rows.disp_count, LANES), f32),
        in_specs=smem(2) + hbm(1) + vmem(7),
        out_specs=vmem(1)[0],
        scratch_shapes=[
            pltpu.VMEM((4, 6 * rows.shell_rows, SUBLANES, LANES), f32),
            pltpu.VMEM((4, tiles, LANES), f32),
            pltpu.VMEM((3, atoms, LANES), f32),
            pltpu.SMEM(tile_block.shape, jnp.int32),
            pltpu.SemaphoreType.DMA(()),
        ],
        compiler_params=params(8),
        cost_estimate=cost(30 * tiles * TILE * TILE, 4 * around.size),
        name="force",
    )(here, active_tile_count, *in_hbm([tile_block]), around, below, above, *own)

    if not whole_slab:
        return by_exchange(rows, strides, around, moves, cross_count)

    constraint_rows = rows.bond_rows + rows.slot_rows
    weight, matrix = pl.pallas_call(
        functools.partial(bond_kernel, rows, domains, strides),
        out_shape=(
            jax.ShapeDtypeStruct((constraint_rows * 3 * domains, LANES), f32),
            jax.ShapeDtypeStruct((domains * rows.matrix, atoms // 2), jnp.bfloat16),
        ),
        in_specs=vmem(1),
        out_specs=tuple(vmem(2)),
        compiler_params=params(16),
        cost_estimate=cost(8 * domains * rows.matrix * atoms // 2, 4 * around.size),
        name="bonds",
    )(around)

    every_move = lax.all_to_all(moves, "dom", 0, 0, tiled=True)

    return pl.pallas_call(
        functools.partial(solve_kernel, rows, domains, strides),
        out_shape=(
            jax.ShapeDtypeStruct(coords.shape, f32),
            jax.ShapeDtypeStruct(coords.shape, f32),
        ),
        in_specs=smem(1) + vmem(4),
        out_specs=tuple(vmem(2)),
        scratch_shapes=[
            pltpu.VMEM((constraint_rows, SUBLANES * domains, LANES), f32),
            pltpu.VMEM((rows.slot_rows, 4 * SUBLANES * domains, LANES), f32),
            pltpu.VMEM((5, rows.atom_rows, SUBLANES * domains, LANES), f32),
        ],
        compiler_params=params(16),
        name="solve",
    )(here, around, every_move, weight, matrix)


def by_exchange(rows, strides, around, moves, cross_count):
    atom_count = rows.atom_rows * LANES
    shell = rows.shell_rows * LANES
    inside = around.reshape(5, rows.count, LANES)

    def flat(at, count):
        return inside[0, at : at + count].reshape(-1)

    def neighbours(at):
        return inside[1:, at : at + rows.shell_rows].reshape(-1)

    coords = jnp.stack([flat(at, rows.atom_rows) for at in rows.coords])
    inv_mass = flat(rows.mass, rows.atom_rows)
    displace = moves[: rows.disp_used].reshape(3, atom_count)
    left = flat(rows.bond_first, rows.bond_rows).astype(jnp.int32)
    right = flat(rows.bond_second, rows.bond_rows).astype(jnp.int32)
    cross_left = flat(rows.cross_first, rows.slot_rows).astype(jnp.int32)
    cross_right = flat(rows.cross_second, rows.slot_rows).astype(jnp.int32)
    side = flat(rows.side, rows.slot_rows).astype(jnp.int32)
    flag = flat(rows.live, rows.slot_rows)
    cross_index = side * shell + cross_right
    far_coords = jnp.stack([neighbours(at) for at in rows.coords])
    far_mass = neighbours(rows.mass)

    def weights(first, second, mass_first, mass_second):
        gap = first - second
        length = jnp.sqrt(jnp.sum(gap * gap, axis=0) + length_floor)
        return gap / length * lax.rsqrt(mass_first + mass_second)

    inner = weights(coords[:, left], coords[:, right], inv_mass[left], inv_mass[right])
    cross = flag * weights(
        coords[:, cross_left], far_coords[:, cross_index], inv_mass[cross_left], far_mass[cross_index]
    )

    def project(field):
        rim = field[:, :shell]
        far = jnp.concatenate([passed_along(rim, "dom", -stride) for stride in strides], axis=1)
        return (
            jnp.sum(inner * (field[:, left] - field[:, right]), axis=0),
            jnp.sum(cross * (field[:, cross_left] - far[:, cross_index]), axis=0),
        )

    def spread(values):
        pushed = inner * values[0]
        pushed_cross = cross * values[1]
        totals = jnp.zeros((3, atom_count), jnp.float32).at[:, left].add(pushed).at[:, right].add(-pushed)
        totals = totals.at[:, cross_left].add(pushed_cross)
        outward = jnp.zeros((3, 4 * shell), jnp.float32).at[:, cross_index].add(-pushed_cross)
        for code, stride in enumerate(strides):
            totals = totals.at[:, :shell].add(
                passed_along(outward[:, code * shell : (code + 1) * shell], "dom", stride)
            )
        return inv_mass * totals

    residue = project(displace)
    summed = residue
    for _ in range(ORDER):
        change = project(spread(residue))
        residue = tuple(now - step for now, step in zip(residue, change))
        summed = tuple(a + b for a, b in zip(summed, residue))
    move = displace - spread(summed)
    return (
        (coords + move).reshape(3, 1, 1, atom_count),
        (move * (1.0 / time_step)).reshape(3, 1, 1, atom_count),
    )


def solution(mesh):
    return jax.shard_map(
        shards,
        mesh=mesh,
        in_specs=(
            P(None, "slab", "dom", None),
            P(None, "slab", "dom", None),
            P("slab", "dom", None),
            P("slab", "dom", None),
            P("slab", "dom", None),
            P("slab", "dom", None, None),
            P("slab", "dom"),
            P(None, "slab", "dom", None),
            P(None, "slab", "dom", None),
            P("slab", "dom", None),
            P("slab", "dom"),
        ),
        out_specs=(P(None, "slab", "dom", None), P(None, "slab", "dom", None)),
        check_vma=False,
    )
```

profile of v0, /device:TPU:0, one launch (start us, length us, event | category | flops | bytes accessed | tf_op | source)
XLA Modules:
  0.0 37.0 jit_solution(6287535433567483964)
XLA Ops:
  1.3 1.5 %pack.1 = (f32[256,128]{1,0:T(8,128)}, f32[8,128]{1,0:T(8,128)S(1)}) custom-call(s32[1,1]{1,0:T(1,128)S(6)} %copy.14.count_ref, f32[3,1,1,512]{3,2,1,0:T(1,128)} %coords_hbm.1, f32[1,1,512]{2,1,0:T(1,128)} %charge_hbm.1, f32[1,1,512]{2,1,0:T(1,128)} %mass_hbm.1, s32[2,1,1,256]{3,2,1,0:T(1,128)} %refs_3_.1, s32[2,1,1,128]{3,2,1,0:T(1,128)} %refs_4_.1, ...), custom_call_target="tpu_custom_call" | custom-call | tf_op jit(solution)/shard_map/pack/pallas_call | solution.py:571
  2.8 7.3 %all-to-all-start = ((f32[8,32,128]{2,1,0:T(8,128)}), f32[8,32,128]{2,1,0:T(8,128)S(1)}, u32[]{:S(2)}, u32[]{:S(2)}) async-start(f32[8,32,128]{2,1,0:T(8,128)} %bitcast.1), calls=%async_computation | async-start | bytes 262144 | tf_op jit(solution)/shard_map/all_to_all | solution.py:604
  10.1 0.7 %collective-permute-start.1 = (f32[8,128]{1,0:T(8,128)S(1)}, f32[8,128]{1,0:T(8,128)S(1)}, u32[]{:S(2)}, u32[]{:S(2)}) collective-permute-start(f32[8,128]{1,0:T(8,128)S(1)} %get-tuple-element.11), channel_id=1, source_target_pairs={{0,24},{8,0},{16,8},{24,16},{1,25},{9,1},{17,9},{25,17},{2,26},{10... | collective-permute-start | bytes 12296 | tf_op jit(solution)/shard_map/ppermute | solution.py:23
  10.7 0.0 collective-permute-start
  11.4 1.5 %own.1 = (f32[4,512,128]{2,1,0:T(8,128)S(1)}, f32[4,64,128]{2,1,0:T(8,128)S(1)}, s32[64,128]{1,0:T(8,128)S(1)}, f32[16,128]{1,0:T(8,128)S(1)}) custom-call(f32[3,1,1,512]{3,2,1,0:T(1,128)} %coords_hbm.1, f32[1,1,512]{2,1,0:T(1,128)} %charge_hbm.1, f32[3,1,1,512]{3,2,1,0:T(1,128)} %velocity_hbm.1, f32[1,1,512]{2,1,0:T(1,128)} %mass_hbm.1, ...), custom_call_target="tpu_custom_call" | custom-call | flops 4194304 | bytes 1048576 | tf_op jit(solution)/shard_map/own/pallas_call | solution.py:585
  12.9 0.0 collective-permute-done.1.above_ref
  12.9 0.8 %collective-permute-done.below_ref = f32[8,128]{1,0:T(8,128)S(1)} collective-permute-done((f32[8,128]{1,0:T(8,128)S(1)}, f32[8,128]{1,0:T(8,128)S(1)}, u32[]{:S(2)}, u32[]{:S(2)}) %collective-permute-start) | collective-permute-done | bytes 4128 | tf_op jit(solution)/shard_map/ppermute | solution.py:23
  13.8 3.7 %all-to-all-done = f32[8,32,128]{2,1,0:T(8,128)S(1)} async-done(((f32[8,32,128]{2,1,0:T(8,128)}), f32[8,32,128]{2,1,0:T(8,128)S(1)}, u32[]{:S(2)}, u32[]{:S(2)}) %all-to-all-start) | async-done | bytes 131104 | tf_op jit(solution)/shard_map/all_to_all | solution.py:604
  17.4 5.2 %force.1 = f32[128,128]{1,0:T(8,128)} custom-call(s32[1]{0:T(128)} %bitcast.here_ref, s32[1,1]{1,0:T(1,128)S(6)} %copy.13.live_ref, s32[1,1,64]{2,1,0:T(1,128)} %block_hbm.1, f32[256,128]{1,0:T(8,128)S(1)} %bitcast.5, f32[8,128]{1,0:T(8,128)S(1)} %collective-permute-done.below_ref, f32[8,128]{1,0:T(8,128)S(1)} %collective-permute-done.1.above_ref, ...), custom_call_target="tpu_custom_call" | custom-call | flops 31457280 | bytes 131072 | tf_op jit(solution)/shard_map/force/pallas_call | solution.py:612
  22.6 3.4 %all-to-all-start.1 = ((f32[8,16,128]{2,1,0:T(8,128)}), f32[8,16,128]{2,1,0:T(8,128)S(1)}, u32[]{:S(2)}, u32[]{:S(2)}) async-start(f32[8,16,128]{2,1,0:T(8,128)} %bitcast.3), calls=%async_computation.1 | async-start | bytes 131072 | tf_op jit(solution)/shard_map/all_to_all | solution.py:646
  26.0 2.7 %bonds.1 = (f32[72,128]{1,0:T(8,128)S(1)}, bf16[6144,256]{1,0:T(8,128)(2,1)S(1)}) custom-call(f32[256,128]{1,0:T(8,128)S(1)} %bitcast.6), custom_call_target="tpu_custom_call" | custom-call | flops 12582912 | bytes 131072 | tf_op jit(solution)/shard_map/bonds/pallas_call | solution.py:633
  28.7 4.2 %all-to-all-done.1 = f32[8,16,128]{2,1,0:T(8,128)S(1)} async-done(((f32[8,16,128]{2,1,0:T(8,128)}), f32[8,16,128]{2,1,0:T(8,128)S(1)}, u32[]{:S(2)}, u32[]{:S(2)}) %all-to-all-start.1) | async-done | bytes 65568 | tf_op jit(solution)/shard_map/all_to_all | solution.py:646
  32.8 4.1 %solve.1 = (f32[3,1,1,512]{3,2,1,0:T(1,128)}, f32[3,1,1,512]{3,2,1,0:T(1,128)}) custom-call(s32[1]{0:T(128)} %bitcast.here_ref, f32[256,128]{1,0:T(8,128)S(1)} %bitcast.7, f32[128,128]{1,0:T(8,128)S(1)} %bitcast.8, f32[72,128]{1,0:T(8,128)S(1)} %get-tuple-element.16.weight_ref, bf16[6144,256]{1,0:T(8,128)(2,1)S(1)} %get-tuple-element.17.matrix_ref), custom_call_target="tpu_custom_call" | custom-call | tf_op jit(solution)/shard_map/solve/pallas_call | solution.py:648
Async XLA Ops:
  2.8 14.6 %all-to-all-start = ((f32[8,32,128]{2,1,0:T(8,128)}), f32[8,32,128]{2,1,0:T(8,128)S(1)}, u32[]{:S(2)}, u32[]{:S(2)}) async-start(f32[8,32,128]{2,1,0:T(8,128)} %bitcast.1), calls=%async_computation | async-start | bytes 262144 | tf_op jit(solution)/shard_map/all_to_all | solution.py:604
  10.1 2.8 %collective-permute-start.1 = (f32[8,128]{1,0:T(8,128)S(1)}, f32[8,128]{1,0:T(8,128)S(1)}, u32[]{:S(2)}, u32[]{:S(2)}) collective-permute-start(f32[8,128]{1,0:T(8,128)S(1)} %get-tuple-element.11), channel_id=1, source_target_pairs={{0,24},{8,0},{16,8},{24,16},{1,25},{9,1},{17,9},{25,17},{2,26},{10... | collective-permute-start | bytes 12296 | tf_op jit(solution)/shard_map/ppermute | solution.py:23
  10.7 3.0 %collective-permute-start = (f32[8,128]{1,0:T(8,128)S(1)}, f32[8,128]{1,0:T(8,128)S(1)}, u32[]{:S(2)}, u32[]{:S(2)}) collective-permute-start(f32[8,128]{1,0:T(8,128)S(1)} %get-tuple-element.11), channel_id=1, source_target_pairs={{0,8},{8,16},{16,24},{24,0},{1,9},{9,17},{17,25},{25,1},{2,10},{10... | collective-permute-start | bytes 12296 | tf_op jit(solution)/shard_map/ppermute | solution.py:23
  22.6 10.2 %all-to-all-start.1 = ((f32[8,16,128]{2,1,0:T(8,128)}), f32[8,16,128]{2,1,0:T(8,128)S(1)}, u32[]{:S(2)}, u32[]{:S(2)}) async-start(f32[8,16,128]{2,1,0:T(8,128)} %bitcast.3), calls=%async_computation.1 | async-start | bytes 131072 | tf_op jit(solution)/shard_map/all_to_all | solution.py:646
where the time goes:
time: 36.9 us; the launch traced here: 37 us
  Pallas kernels  15 us (41%)
  starting transfers between devices  11.3 us (31%)
  waiting for transfers between devices  8.66 us (23%)
  between operations  1.98 us (5%)
    all_to_all x1, starting transfers between devices, shards(): around = lax.all_to_all(packed, 'dom', 0, 0, tiled=True)  7.29 us
    pallas_call x1, Pallas kernels, shards(): pl.pallas_call(functools.partial(force_kernel, rows, copies, holders), ou...  5.18 us
    all_to_all x1, waiting for transfers between devices, shards(): every_move = lax.all_to_all(moves, 'dom', 0, 0, tiled=True)  4.17 us
    pallas_call x1, Pallas kernels, shards(): pl.pallas_call(functools.partial(solve_kernel, rows, domains, strides), o...  4.13 us
    all_to_all x1, waiting for transfers between devices, shards(): around = lax.all_to_all(packed, 'dom', 0, 0, tiled=True)  3.66 us
    all_to_all x1, starting transfers between devices, shards(): every_move = lax.all_to_all(moves, 'dom', 0, 0, tiled=True)  3.36 us
    pallas_call x1, Pallas kernels, shards(): pl.pallas_call(functools.partial(bond_kernel, rows, domains, strides), ou...  2.66 us
    pallas_call x1, Pallas kernels, shards(): pl.pallas_call(functools.partial(own_kernel, rows), out_shape=(jax.ShapeD...  1.53 us
  transfers between devices with their start and end apart: 4, of which 3 were waited for; matrix products, arithmetic and copies ran while one was open for 0% of the time, Pallas kernels for 11%

commit v1 on v0

--- a/solution.py
+++ b/solution.py
@@ -57,8 +57,6 @@
         at += self.slot_rows
         self.side = at
         at += self.slot_rows
-        self.live = at
-        at += self.slot_rows
         self.used = at
         self.count = round_up(at, SUBLANES)
         self.shell_terms = (self.bond_rows + self.slot_rows) * LANES
@@ -66,7 +64,8 @@
         self.cross_at = self.bond_rows * LANES
         self.far_at = self.shell_terms + self.bond_rows * LANES
         self.matrix = self.far_at + self.slot_rows * LANES
-        self.disp_used = 3 * self.atom_rows
+        self.live = 3 * self.atom_rows
+        self.disp_used = self.live + self.slot_rows
         self.disp_count = round_up(self.disp_used, SUBLANES)
 
 
@@ -90,7 +89,7 @@
     return copies
 
 
-def pack_kernel(rows, copies, count_ref, *refs):
+def pack_kernel(rows, copies, *refs):
     sources, (out_ref, rim_ref), targets, sem_ref = refs[:6], refs[6:8], refs[8:14], refs[14]
     for copy in fetched(sources, targets, sem_ref):
         copy.wait()
@@ -114,10 +113,7 @@
     put(rows.bond_second, bonds_ref[1, 0].astype(jnp.float32))
     put(rows.cross_first, cross_ref[0, 0].astype(jnp.float32))
     put(rows.cross_second, cross_ref[1, 0].astype(jnp.float32))
-    side = side_ref[0]
-    put(rows.side, side.astype(jnp.float32))
-    slot = lax.broadcasted_iota(jnp.int32, side.shape, 1)
-    put(rows.live, jnp.where(slot < count_ref[0, 0], 1.0, 0.0))
+    put(rows.side, side_ref[0].astype(jnp.float32))
     if rows.count > rows.used:
         for copy in range(copies):
             out_ref[pl.ds(copy * rows.count + rows.used, rows.count - rows.used), :] = jnp.zeros(
@@ -127,7 +123,7 @@
 
 SHRINK = 1.0 / 4.0
 OUT_OF_REACH = 1000.0
-TILES_STEP = 2
+TILES_STEP = 4
 
 
 def own_kernel(
@@ -189,9 +185,9 @@
 def force_kernel(
     rows,
     copies,
-    holders,
-    here_ref,
+    place,
     live_ref,
+    count_ref,
     block_hbm,
     around_ref,
     below_ref,
@@ -211,10 +207,9 @@
     tiles = index_ref.shape[0]
     block_copy = pltpu.make_async_copy(block_hbm, block_ref, sem_ref)
     block_copy.start()
-    me = here_ref[0]
+    holders = place()
     starts = [rows.coords[0], rows.coords[1], rows.coords[2], rows.charge]
     entry_rows = 6 * shell_rows
-    blocks = around_ref.shape[0] // rows.count
 
     def broadcast(row):
         return jnp.broadcast_to(row, (SUBLANES, LANES))
@@ -223,7 +218,7 @@
         factor = SHRINK if c < 3 else 1.0
         at = 0
         for neighbour in range(4):
-            base = lax.rem(me + holders[neighbour], blocks) * rows.count + starts[c]
+            base = holders[neighbour] * rows.count + starts[c]
             for part in range(shell_rows):
                 table_ref[c, at] = broadcast(around_ref[pl.ds(base + part, 1), :] * factor)
                 at += 1
@@ -250,6 +245,8 @@
     sum_ref[...] = jnp.zeros(sum_ref.shape, jnp.float32)
     block_copy.wait()
 
+    softening = 1.0 / cutoff_sq
+
     def add_tile(tile):
         base = block_ref[0, 0, tile] * TILE
         far = [broadcast(far_ref[c, pl.ds(tile, 1), :]) for c in range(4)]
@@ -257,8 +254,8 @@
             at = pl.ds(pl.multiple_of(base + group * SUBLANES, SUBLANES), SUBLANES)
             gap = [own_ref[c, at, :] - far[c] for c in range(3)]
             square = gap[0] * gap[0] + gap[1] * gap[1] + gap[2] * gap[2]
-            inverse = pl.reciprocal(square + 1.0 / cutoff_sq, approx=True)
-            weight = inverse * jnp.maximum(1.0 - square, 0.0)
+            inverse = pl.reciprocal(square + softening, approx=True)
+            weight = jnp.maximum(inverse - 1.0 / (1.0 + softening), 0.0)
             strength = (inverse - own_ref[3, at, :] * far[3]) * (weight * weight)
             for c in range(3):
                 sum_ref[c, at, :] = sum_ref[c, at, :] + strength * gap[c]
@@ -270,7 +267,7 @@
 
     lax.fori_loop(0, lax.div(live + TILES_STEP - 1, TILES_STEP), add_tiles, 0)
 
-    scale = time_step * time_step * force_scale * 4.0 / 2048.0
+    scale = time_step * time_step * force_scale * 4.0 / 2048.0 * (1.0 + softening) ** 2
 
     def lane_sums(c, part):
         return jnp.sum(sum_ref[c, pl.ds(part * LANES, LANES), :].T, axis=0, keepdims=True)
@@ -282,6 +279,11 @@
             moved = time_step * speed + scale * lane_sums(c, part) * mass
             for copy in range(copies):
                 out_ref[pl.ds(copy * rows.disp_count + c * atom_rows + part, 1), :] = moved
+    slot = lax.broadcasted_iota(jnp.int32, (1, LANES), 1)
+    for part in range(rows.slot_rows):
+        flag = jnp.where(slot + part * LANES < count_ref[0, 0], 1.0, 0.0)
+        for copy in range(copies):
+            out_ref[pl.ds(copy * rows.disp_count + rows.live + part, 1), :] = flag
     if rows.disp_count > rows.disp_used:
         for copy in range(copies):
             out_ref[pl.ds(copy * rows.disp_count + rows.disp_used, rows.disp_count - rows.disp_used), :] = jnp.zeros(
@@ -318,7 +320,6 @@
         first = index(rows.cross_first + part)
         second = index(rows.cross_second + part)
         side = load(rows.side + part)
-        live = load(rows.live + part)
         other = [jnp.zeros((domains, LANES), jnp.float32) for _ in range(4)]
         for code, stride in enumerate(strides):
             seen = pltpu.roll(second, stride % domains, 0)
@@ -327,7 +328,7 @@
                 other[f] = jnp.where(side == code, value, other[f])
         values = weights([pick(f[:shell_rows], first) for f in fields], other, at)
         for c in range(3):
-            weight_ref[pl.ds((at * 3 + c) * domains, domains), :] = values[c] * live
+            weight_ref[pl.ds((at * 3 + c) * domains, domains), :] = values[c]
         at += 1
 
     down = lax.broadcasted_iota(jnp.int32, (SUBLANES, LANES), 0)
@@ -375,7 +376,6 @@
     rows,
     domains,
     strides,
-    here_ref,
     around_ref,
     moves_ref,
     weight_ref,
@@ -388,7 +388,7 @@
 ):
     atom_rows, shell_rows = rows.atom_rows, rows.shell_rows
     bond_rows, slot_rows = rows.bond_rows, rows.slot_rows
-    me = here_ref[0]
+    me = lax.axis_index("dom")
 
     def load(row):
         return around_ref[pl.ds(row, domains, stride=rows.count), :]
@@ -403,8 +403,14 @@
     sides = [load(rows.side + p) for p in range(slot_rows)]
     masses = [load(rows.mass + p) for p in range(atom_rows)]
 
+    def move_rows(row):
+        return moves_ref[pl.ds(row, domains, stride=rows.disp_count), :]
+
     def weight(at, c):
-        return weight_ref[pl.ds((at * 3 + c) * domains, domains), :]
+        value = weight_ref[pl.ds((at * 3 + c) * domains, domains), :]
+        return value if at < bond_rows else value * live[at - bond_rows]
+
+    live = [move_rows(rows.live + p) for p in range(slot_rows)]
 
     def project(fields):
         result = []
@@ -486,7 +492,7 @@
         return [[field(c, part) for part in range(atom_rows)] for c in range(3)]
 
     moves = [
-        [moves_ref[pl.ds(c * atom_rows + p, domains, stride=rows.disp_count), :] for p in range(atom_rows)]
+        [move_rows(c * atom_rows + p) for p in range(atom_rows)]
         for c in range(3)
     ]
     push_ref[...] = jnp.zeros(push_ref.shape, jnp.float32)
@@ -574,12 +580,12 @@
             jax.ShapeDtypeStruct((copies * rows.count, LANES), f32),
             jax.ShapeDtypeStruct((4 * rows.shell_rows, LANES), f32),
         ),
-        in_specs=smem(1) + hbm(len(sent)),
+        in_specs=hbm(len(sent)),
         out_specs=tuple(vmem(2)),
         scratch_shapes=room_for(sent) + [pltpu.SemaphoreType.DMA((len(sent),))],
         compiler_params=params(4),
         name="pack",
-    )(cross_count, *in_hbm(sent))
+    )(*in_hbm(sent))
 
     alone = (coords, charge, velocity, inv_mass, tile_atoms)
     own = pl.pallas_call(
@@ -602,15 +608,20 @@
     above = passed_along(rim, "slab", -1)
     if whole_slab:
         around = lax.all_to_all(packed, "dom", 0, 0, tiled=True)
-        here = lax.axis_index("dom").reshape(1)
-        holders = [stride % domains for stride in strides]
+
+        def place():
+            me = lax.axis_index("dom")
+            return [lax.rem(me + stride % domains, domains) for stride in strides]
+
     else:
         around = jnp.concatenate([packed] + [passed_along(packed, "dom", -stride) for stride in strides], axis=0)
-        here = jnp.zeros(1, jnp.int32)
-        holders = [1, 2, 3, 4]
+
+        def place():
+            return [1, 2, 3, 4]
+
 
     moves = pl.pallas_call(
-        functools.partial(force_kernel, rows, copies, holders),
+        functools.partial(force_kernel, rows, copies, place),
         out_shape=jax.ShapeDtypeStruct((copies * rows.disp_count, LANES), f32),
         in_specs=smem(2) + hbm(1) + vmem(7),
         out_specs=vmem(1)[0],
@@ -624,7 +635,7 @@
         compiler_params=params(8),
         cost_estimate=cost(30 * tiles * TILE * TILE, 4 * around.size),
         name="force",
-    )(here, active_tile_count, *in_hbm([tile_block]), around, below, above, *own)
+    )(active_tile_count, cross_count, *in_hbm([tile_block]), around, below, above, *own)
 
     if not whole_slab:
         return by_exchange(rows, strides, around, moves, cross_count)
@@ -651,7 +662,7 @@
             jax.ShapeDtypeStruct(coords.shape, f32),
             jax.ShapeDtypeStruct(coords.shape, f32),
         ),
-        in_specs=smem(1) + vmem(4),
+        in_specs=vmem(4),
         out_specs=tuple(vmem(2)),
         scratch_shapes=[
             pltpu.VMEM((constraint_rows, SUBLANES * domains, LANES), f32),
@@ -660,7 +671,7 @@
         ],
         compiler_params=params(16),
         name="solve",
-    )(here, around, every_move, weight, matrix)
+    )(around, every_move, weight, matrix)
 
 
 def by_exchange(rows, strides, around, moves, cross_count):
@@ -676,13 +687,13 @@
 
     coords = jnp.stack([flat(at, rows.atom_rows) for at in rows.coords])
     inv_mass = flat(rows.mass, rows.atom_rows)
-    displace = moves[: rows.disp_used].reshape(3, atom_count)
+    displace = moves[: rows.live].reshape(3, atom_count)
     left = flat(rows.bond_first, rows.bond_rows).astype(jnp.int32)
     right = flat(rows.bond_second, rows.bond_rows).astype(jnp.int32)
     cross_left = flat(rows.cross_first, rows.slot_rows).astype(jnp.int32)
     cross_right = flat(rows.cross_second, rows.slot_rows).astype(jnp.int32)
     side = flat(rows.side, rows.slot_rows).astype(jnp.int32)
-    flag = flat(rows.live, rows.slot_rows)
+    flag = moves[rows.live : rows.disp_used].reshape(-1)
     cross_index = side * shell + cross_right
     far_coords = jnp.stack([neighbours(at) for at in rows.coords])
     far_mass = neighbours(rows.mass)

time: 36.9 us -> 36.1 us (0.978)
  waiting for transfers between devices: 8.66 us -> 8.02 us
    ppermute x2, waiting for transfers between devices: 0.83 us -> 0.18 us  [passed_along(): lax.ppermute(array, axis, [(i, (i + by) % length) for i in range(length)])]
  transfers between devices with their start and end apart: 4 -> 4, of which waited for: 3 -> 3; matrix products, arithmetic and copies ran while one was open for 0% -> 0% of each run, Pallas kernels for 11% -> 12%
where the time goes in v1:
time: 36.1 us; the launch traced here: 36 us
  Pallas kernels  14.7 us (41%)
  starting transfers between devices  11.3 us (31%)
  waiting for transfers between devices  8.02 us (22%)
  between operations  1.98 us (5%)
    all_to_all x1, starting transfers between devices, shards(): around = lax.all_to_all(packed, 'dom', 0, 0, tiled=True)  7.29 us
    pallas_call x1, Pallas kernels, shards(): pl.pallas_call(functools.partial(force_kernel, rows, copies, place), out_...  4.89 us
    all_to_all x1, waiting for transfers between devices, shards(): every_move = lax.all_to_all(moves, 'dom', 0, 0, tiled=True)  4.17 us
    pallas_call x1, Pallas kernels, shards(): pl.pallas_call(functools.partial(solve_kernel, rows, domains, strides), o...  4.12 us
    all_to_all x1, waiting for transfers between devices, shards(): around = lax.all_to_all(packed, 'dom', 0, 0, tiled=True)  3.66 us
    all_to_all x1, starting transfers between devices, shards(): every_move = lax.all_to_all(moves, 'dom', 0, 0, tiled=True)  3.36 us
    pallas_call x1, Pallas kernels, shards(): pl.pallas_call(functools.partial(bond_kernel, rows, domains, strides), ou...  2.66 us
    pallas_call x1, Pallas kernels, shards(): pl.pallas_call(functools.partial(own_kernel, rows), out_shape=(jax.ShapeD...  1.53 us
  transfers between devices with their start and end apart: 4, of which 3 were waited for; matrix products, arithmetic and copies ran while one was open for 0% of the time, Pallas kernels for 12%

profile of v1, /device:TPU:0, one launch (start us, length us, event | category | flops | bytes accessed | tf_op | source)
XLA Modules:
  0.0 36.0 jit_solution(11456510464337834368)
XLA Ops:
  0.6 1.5 %pack.1 = (f32[256,128]{1,0:T(8,128)}, f32[8,128]{1,0:T(8,128)S(1)}) custom-call(f32[3,1,1,512]{3,2,1,0:T(1,128)} %coords_hbm.1, f32[1,1,512]{2,1,0:T(1,128)} %charge_hbm.1, f32[1,1,512]{2,1,0:T(1,128)} %mass_hbm.1, s32[2,1,1,256]{3,2,1,0:T(1,128)} %refs_3_.1, s32[2,1,1,128]{3,2,1,0:T(1,128)} %refs_4_.1, s32[1,1,128]{2,1,0:T(1,128)} %refs_5_.1), custom_call_target="tpu_custom_call" | custom-call | tf_op jit(solution)/shard_map/pack/pallas_call | solution.py:577
  2.2 7.3 %all-to-all-start = ((f32[8,32,128]{2,1,0:T(8,128)}), f32[8,32,128]{2,1,0:T(8,128)S(1)}, u32[]{:S(2)}, u32[]{:S(2)}) async-start(f32[8,32,128]{2,1,0:T(8,128)} %bitcast), calls=%async_computation | async-start | bytes 262144 | tf_op jit(solution)/shard_map/all_to_all | solution.py:610
  9.4 0.7 %collective-permute-start.1 = (f32[8,128]{1,0:T(8,128)S(1)}, f32[8,128]{1,0:T(8,128)S(1)}, u32[]{:S(2)}, u32[]{:S(2)}) collective-permute-start(f32[8,128]{1,0:T(8,128)S(1)} %get-tuple-element.11), channel_id=1, source_target_pairs={{0,24},{8,0},{16,8},{24,16},{1,25},{9,1},{17,9},{25,17},{2,26},{10... | collective-permute-start | bytes 12296 | tf_op jit(solution)/shard_map/ppermute | solution.py:23
  10.1 0.0 collective-permute-start
  11.4 1.5 %own.1 = (f32[4,512,128]{2,1,0:T(8,128)S(1)}, f32[4,64,128]{2,1,0:T(8,128)S(1)}, s32[64,128]{1,0:T(8,128)S(1)}, f32[16,128]{1,0:T(8,128)S(1)}) custom-call(f32[3,1,1,512]{3,2,1,0:T(1,128)} %coords_hbm.1, f32[1,1,512]{2,1,0:T(1,128)} %charge_hbm.1, f32[3,1,1,512]{3,2,1,0:T(1,128)} %velocity_hbm.1, f32[1,1,512]{2,1,0:T(1,128)} %mass_hbm.1, ...), custom_call_target="tpu_custom_call" | custom-call | flops 4194304 | bytes 1048576 | tf_op jit(solution)/shard_map/own/pallas_call | solution.py:591
  12.9 0.0 collective-permute-done.1.above_ref
  12.9 0.2 collective-permute-done.below_ref
  13.1 3.7 %all-to-all-done = f32[8,32,128]{2,1,0:T(8,128)S(1)} async-done(((f32[8,32,128]{2,1,0:T(8,128)}), f32[8,32,128]{2,1,0:T(8,128)S(1)}, u32[]{:S(2)}, u32[]{:S(2)}) %all-to-all-start) | async-done | bytes 131104 | tf_op jit(solution)/shard_map/all_to_all | solution.py:610
  16.8 4.9 %force.1 = f32[128,128]{1,0:T(8,128)} custom-call(s32[1,1]{1,0:T(1,128)S(6)} %copy.13.live_ref, s32[1,1]{1,0:T(1,128)S(6)} %copy.14.count_ref, s32[1,1,64]{2,1,0:T(1,128)} %block_hbm.1, f32[256,128]{1,0:T(8,128)S(1)} %bitcast.4, f32[8,128]{1,0:T(8,128)S(1)} %collective-permute-done.below_ref, f32[8,128]{1,0:T(8,128)S(1)} %collective-permute-done.1.above_ref, ...), custom_call_target="tpu_custom_call" | custom-call | flops 31457280 | bytes 131072 | tf_op jit(solution)/shard_map/force/pallas_call | solution.py:623
  21.7 3.4 %all-to-all-start.1 = ((f32[8,16,128]{2,1,0:T(8,128)}), f32[8,16,128]{2,1,0:T(8,128)S(1)}, u32[]{:S(2)}, u32[]{:S(2)}) async-start(f32[8,16,128]{2,1,0:T(8,128)} %bitcast.2), calls=%async_computation.1 | async-start | bytes 131072 | tf_op jit(solution)/shard_map/all_to_all | solution.py:657
  25.1 2.7 %bonds.1 = (f32[72,128]{1,0:T(8,128)S(1)}, bf16[6144,256]{1,0:T(8,128)(2,1)S(1)}) custom-call(f32[256,128]{1,0:T(8,128)S(1)} %bitcast.5), custom_call_target="tpu_custom_call" | custom-call | flops 12582912 | bytes 131072 | tf_op jit(solution)/shard_map/bonds/pallas_call | solution.py:644
  27.7 4.2 %all-to-all-done.1 = f32[8,16,128]{2,1,0:T(8,128)S(1)} async-done(((f32[8,16,128]{2,1,0:T(8,128)}), f32[8,16,128]{2,1,0:T(8,128)S(1)}, u32[]{:S(2)}, u32[]{:S(2)}) %all-to-all-start.1) | async-done | bytes 65568 | tf_op jit(solution)/shard_map/all_to_all | solution.py:657
  31.9 4.1 %solve.1 = (f32[3,1,1,512]{3,2,1,0:T(1,128)}, f32[3,1,1,512]{3,2,1,0:T(1,128)}) custom-call(f32[256,128]{1,0:T(8,128)S(1)} %bitcast.6, f32[128,128]{1,0:T(8,128)S(1)} %bitcast.7, f32[72,128]{1,0:T(8,128)S(1)} %get-tuple-element.16.weight_ref, bf16[6144,256]{1,0:T(8,128)(2,1)S(1)} %get-tuple-element.17.matrix_ref), custom_call_target="tpu_custom_call" | custom-call | tf_op jit(solution)/shard_map/solve/pallas_call | solution.py:659
Async XLA Ops:
  2.2 14.6 %all-to-all-start = ((f32[8,32,128]{2,1,0:T(8,128)}), f32[8,32,128]{2,1,0:T(8,128)S(1)}, u32[]{:S(2)}, u32[]{:S(2)}) async-start(f32[8,32,128]{2,1,0:T(8,128)} %bitcast), calls=%async_computation | async-start | bytes 262144 | tf_op jit(solution)/shard_map/all_to_all | solution.py:610
  9.4 3.5 %collective-permute-start.1 = (f32[8,128]{1,0:T(8,128)S(1)}, f32[8,128]{1,0:T(8,128)S(1)}, u32[]{:S(2)}, u32[]{:S(2)}) collective-permute-start(f32[8,128]{1,0:T(8,128)S(1)} %get-tuple-element.11), channel_id=1, source_target_pairs={{0,24},{8,0},{16,8},{24,16},{1,25},{9,1},{17,9},{25,17},{2,26},{10... | collective-permute-start | bytes 12296 | tf_op jit(solution)/shard_map/ppermute | solution.py:23
  10.1 3.0 %collective-permute-start = (f32[8,128]{1,0:T(8,128)S(1)}, f32[8,128]{1,0:T(8,128)S(1)}, u32[]{:S(2)}, u32[]{:S(2)}) collective-permute-start(f32[8,128]{1,0:T(8,128)S(1)} %get-tuple-element.11), channel_id=1, source_target_pairs={{0,8},{8,16},{16,24},{24,0},{1,9},{9,17},{17,25},{25,1},{2,10},{10... | collective-permute-start | bytes 12296 | tf_op jit(solution)/shard_map/ppermute | solution.py:23
  21.7 10.2 %all-to-all-start.1 = ((f32[8,16,128]{2,1,0:T(8,128)}), f32[8,16,128]{2,1,0:T(8,128)S(1)}, u32[]{:S(2)}, u32[]{:S(2)}) async-start(f32[8,16,128]{2,1,0:T(8,128)} %bitcast.2), calls=%async_computation.1 | async-start | bytes 131072 | tf_op jit(solution)/shard_map/all_to_all | solution.py:657
